TPU v7x, 512 devices: a whole 4x4x16 slice. The times are simulated.
512 devices in a mesh: lat: 8 (over x, core), lon: 64 (over y, z).
Axes of the slice: x: 4, y: 4, z: 16, core: 2. Of those that a mesh axis runs over, the one named last changes fastest.
Arguments:
- rhs: float32 [8, 64, 6, 16, 256], P('lat', 'lon')
- precond: float32 [8, 64, 6, 256], P('lat', 'lon'), may hold values from 0.3 to 1
- factor: bfloat16 [8, 64, 6, 256, 256], P('lat', 'lon')
- kriging: bfloat16 [8, 64, 6, 4, 256, 256], P('lat', 'lon'), may hold values from -0.1875 to 0.1875
- neighbours: int32 [8, 64, 6, 4], P('lat', 'lon'), may hold values from 0 to 3071, as said below
- owner: int32 [3072], replicated, may hold values from 0 to 3071, as said below
- counts: int32 [8, 64], P('lat', 'lon'), may hold values from 1 to 6, as said below
Outputs:
- solution: float32 [8, 64, 6, 16, 256], P('lat', 'lon')
- residual: float32 [8, 64, 6, 16, 256], P('lat', 'lon')
Inputs may be any that keep to these rules, and one draw needn't show every extreme that they name: `counts`: each region holds 1 to 6 blocks in its first slots; some region holds 6. `owner`: a permutation of 0 to 3071; block id g lives in slot owner[g] % 6 of region owner[g] // 6. `neighbours`: ids of live blocks in the same region or one of its eight adjacent regions, adjacency periodic in longitude and not in latitude.
All inputs are finite; a program needn't handle non-finite values.
Results may differ from a plain program's by a relative error of at most 0.025.
Values may be sent and summed in bfloat16 or wider, within the bound.
A program may use at most 64 MiB of HBM per device.

v0:
```python
import jax
import jax.numpy as jnp
from jax import lax
from jax.sharding import PartitionSpec as P

ITERS = 2
nugget = 1.0


def from_behind(block, axis, distance):
    devices = range(lax.axis_size(axis))
    route = [((i - distance) % len(devices), i) for i in devices]
    return lax.ppermute(block, axis, route)


def from_behind_2(value, axis, steps):
    count = lax.axis_size(axis)
    leading, last = (max(0, -steps), min(count, count - steps))
    return lax.ppermute(value, axis, [(source, source + steps) for source in range(leading, last)])


def with_halo(block, sides, width):
    for axis, dim in sides:
        count = lax.axis_size(axis)
        forward = [(i, i + 1) for i in range(count - 1)]
        forward.append((count - 1, 0))
        backward = [(target, source) for source, target in forward]
        low = lax.ppermute(
            lax.slice_in_dim(block, block.shape[dim] - width, None, axis=dim), axis, forward
        )
        high = lax.ppermute(lax.slice_in_dim(block, 0, width, axis=dim), axis, backward)
        block = jnp.concatenate([low, block, high], axis=dim)
    return block


def inner(first, second):
    return jnp.sum(first * second, axis=(0, 1, 2, 4))


def lon_back(values, offset):
    return from_behind(values.astype(jnp.bfloat16), "lon", offset).astype(values.dtype)


def lat_back(values, offset):
    return from_behind_2(values.astype(jnp.bfloat16), "lat", offset).astype(values.dtype)


def body(rhs, precond, factor, kriging, neighbours, owner, counts):
    slots = factor.shape[2]
    samples = rhs.shape[3]
    width = rhs.shape[4]
    links = kriging.shape[3]
    sectors = lax.axis_size("lon")
    my_lat = lax.axis_index("lat")
    my_lon = lax.axis_index("lon")
    live = (jnp.arange(slots) < counts[0, 0]).astype(jnp.float32)
    source = rhs * live[None, None, :, None, None]
    scaling = precond[:, :, :, None, :]
    position = owner[neighbours[0, 0]]
    region = position // slots
    slot = position % slots
    step_lat = region // sectors - my_lat
    step_lon = (region % sectors - my_lon + 1) % sectors - 1
    local = ((step_lat + 1) * 3 + step_lon + 1) * slots + slot
    target = (jnp.arange(9 * slots)[:, None] == local.reshape(-1)[None, :]).astype(jnp.float32)
    weights = kriging[0, 0]
    blocks = factor[0, 0]
    solution = jnp.zeros_like(source)
    residual = source

    def residual_total(first, second):
        return lax.psum(inner(first, second), ("lat", "lon"))

    preconditioned = scaling * residual
    direction = preconditioned
    current = residual_total(residual, preconditioned)
    for step in range(ITERS):
        rounded = direction.astype(jnp.bfloat16)
        beside_all = with_halo(rounded, (("lat", 0), ("lon", 1)), 1)
        panel = beside_all.reshape(9 * slots, samples, width)[local]
        lifted = rounded[0, 0].astype(jnp.float32) - jnp.einsum(
            "knij,knsj->ksi", weights, panel, preferred_element_type=jnp.float32
        )
        lifted = lifted.astype(jnp.bfloat16)
        whitened = (
            jnp.einsum("kij,ksj->ksi", blocks, lifted, preferred_element_type=jnp.float32)
            * live[:, None, None]
        )
        whitened = whitened.astype(jnp.bfloat16)
        back = jnp.einsum("kji,ksj->ksi", blocks, whitened, preferred_element_type=jnp.float32)
        spread = -jnp.einsum(
            "knji,ksj->knsi", weights, back.astype(jnp.bfloat16), preferred_element_type=jnp.float32
        )
        placed = jnp.dot(
            target, spread.reshape(slots * links, samples * width), precision=lax.Precision.HIGHEST
        )
        placed = placed.reshape(3, 3, slots, samples, width)
        middle = placed[:, 1] + lon_back(placed[:, 2], 1) + lon_back(placed[:, 0], -1)
        total = middle[1] + lat_back(middle[2], 1) + lat_back(middle[0], -1)
        image = (back + total)[None, None] + nugget * direction
        alpha = current / lax.psum(inner(direction, image), ("lat", "lon"))
        solution = solution + alpha[:, None] * direction
        residual = residual - alpha[:, None] * image
        if step + 1 < ITERS:
            preconditioned = scaling * residual
            following = residual_total(residual, preconditioned)
            direction = preconditioned + (following / current)[:, None] * direction
            current = following
    return (solution, residual)


def solution(mesh):
    return jax.shard_map(
        body,
        mesh=mesh,
        in_specs=(
            P("lat", "lon", None, None, None),
            P("lat", "lon", None, None),
            P("lat", "lon", None, None, None),
            P("lat", "lon", None, None, None, None),
            P("lat", "lon", None, None),
            P(),
            P("lat", "lon"),
        ),
        out_specs=(P("lat", "lon", None, None, None), P("lat", "lon", None, None, None)),
        check_vma=False,
    )
```

profile of v0, /device:TPU:1, one launch (start us, length us, event | category | flops | bytes accessed | tf_op | source)
XLA Modules:
  0.0 421.8 jit_solution(18384698949551810775)
XLA Ops:
  1.5 0.8 copy.60
  2.3 1.0 multiply_convert_fusion
  3.3 6.9 %collective-permute-start.1 = (bf16[1,1,6,16,256]{4,3,2,1,0:T(8,128)(2,1)S(1)}, bf16[1,1,6,16,256]{4,3,2,1,0:T(8,128)(2,1)S(1)}, u32[]{:S(2)}, u32[]{:S(2)}) collective-permute-start(bf16[1,1,6,16,256]{4,3,2,1,0:T(8,128)(2,1)S(1)} %multiply_convert_fusion), channel_id=1, source_target_pairs={{64,0},{128,64},{192,128},{256,192},{320,256},{384,320},{448,384},... | collective-permute-start | bytes 147464 | tf_op jit(solution)/shard_map/ppermute | solution.py:31
  10.2 0.7 compare_select_fusion.1
  10.8 0.1 copy.22
  10.9 0.1 reshape.384
  11.0 1.4 gather_fusion
  12.4 0.1 ne.150
  12.5 0.1 copy.24
  12.8 0.1 copy.25
  12.9 0.1 copy.23
  13.1 0.1 copy.30
  13.2 0.1 reshape.392
  13.3 9.3 %collective-permute-start.3 = (bf16[3,1,6,16,256]{4,3,2,1,0:T(8,128)(2,1)S(1)}, bf16[3,1,6,16,256]{4,3,2,1,0:T(8,128)(2,1)S(1)}, u32[]{:S(2)}, u32[]{:S(2)}) collective-permute-start(bf16[3,1,6,16,256]{4,3,2,1,0:T(8,128)(2,1)S(1)} %pad_maximum_fusion.2), channel_id=1, source_target_pairs={{1,0},{2,1},{3,2},{4,3},{5,4},{6,5},{7,6},{8,7},{9,8},{10,9},{11,1... | collective-permute-start | bytes 442376 | tf_op jit(solution)/shard_map/ppermute | solution.py:31
  22.6 1.9 collective-permute-start.2
  24.6 0.1 collective-permute-done.3
  24.7 7.1 %collective-permute-done.2 = bf16[3,1,6,16,256]{4,3,2,1,0:T(8,128)(2,1)S(1)} collective-permute-done((bf16[3,1,6,16,256]{4,3,2,1,0:T(8,128)(2,1)S(1)}, bf16[3,1,6,16,256]{4,3,2,1,0:T(8,128)(2,1)S(1)}, u32[]{:S(2)}, u32[]{:S(2)}) %collective-permute-start.2) | collective-permute-done | bytes 147488 | tf_op jit(solution)/shard_map/ppermute | solution.py:28
  31.8 0.8 pad_maximum_fusion
  32.6 1.6 gather_fusion.1
  34.2 0.9 fusion.26
  35.2 1.8 fusion.35
  37.0 0.5 fusion.8
  37.5 0.9 fusion.42
  38.4 0.3 fusion.99
  38.7 1.9 collective-permute-start.4
  40.7 6.7 %collective-permute-start.5 = (bf16[3,6,16,256]{3,2,1,0:T(8,128)(2,1)S(1)}, bf16[3,6,16,256]{3,2,1,0:T(8,128)(2,1)S(1)}, u32[]{:S(2)}, u32[]{:S(2)}) collective-permute-start(bf16[3,6,16,256]{3,2,1,0:T(8,128)(2,1)S(1)} %get-tuple-element.21), channel_id=1, source_target_pairs={{1,0},{2,1},{3,2},{4,3},{5,4},{6,5},{7,6},{8,7},{9,8},{10,9},{11,1... | collective-permute-start | bytes 442376 | tf_op jit(solution)/shard_map/ppermute | solution.py:13
  47.4 0.6 collective-permute-done.4
  48.0 1.5 collective-permute-done.5
  49.5 6.7 %collective-permute-start.6 = (bf16[6,16,256]{2,1,0:T(8,128)(2,1)S(1)}, bf16[6,16,256]{2,1,0:T(8,128)(2,1)S(1)}, u32[]{:S(2)}, u32[]{:S(2)}) collective-permute-start(bf16[6,16,256]{2,1,0:T(8,128)(2,1)S(1)} %get-tuple-element.26), channel_id=1, source_target_pairs={{0,64},{64,128},{128,192},{192,256},{256,320},{320,384},{384,448},... | collective-permute-start | bytes 147464 | tf_op jit(solution)/shard_map/ppermute | solution.py:19
  56.3 1.9 collective-permute-start.7
  58.2 3.5 collective-permute-done.7
  61.7 0.2 fusion.49
  61.9 102.7 %all-reduce = (f32[16]{0:T(128)S(1)}, f32[16]{0:T(128)S(1)}) all-reduce(f32[16]{0:T(128)S(1)} %get-tuple-element.3, f32[16]{0:T(128)S(1)} %get-tuple-element.2), channel_id=1, replica_groups=mesh['lat'=8,'lon'=64] {'lat','lon'}, use_global_device_ids=true, to_apply=%region_1.2 | all-reduce | flops 32 | bytes 256 | tf_op jit(solution)/shard_map/psum | solution.py:72
  164.6 0.5 copy-done.17
  165.1 1.6 fusion.51
  166.7 99.2 %psum.30 = f32[16]{0:T(128)S(1)} all-reduce(f32[16]{0:T(128)} %get-tuple-element.10), channel_id=1, replica_groups=mesh['lat'=8,'lon'=64] {'lat','lon'}, use_global_device_ids=true, to_apply=%region_5.6 | all-reduce | flops 16 | bytes 128 | tf_op jit(solution)/shard_map/psum | solution.py:72
  266.0 0.6 div.56
  266.6 0.6 copy-done.12
  267.2 0.7 fusion.93
  267.9 0.7 collective-permute-start.9
  268.5 1.1 collective-permute-start.8
  269.6 1.8 collective-permute-done.9
  271.4 5.3 %collective-permute-start.11 = (bf16[3,1,6,16,256]{4,3,2,1,0:T(8,128)(2,1)S(1)}, bf16[3,1,6,16,256]{4,3,2,1,0:T(8,128)(2,1)S(1)}, u32[]{:S(2)}, u32[]{:S(2)}) collective-permute-start(bf16[3,1,6,16,256]{4,3,2,1,0:T(8,128)(2,1)S(1)} %pad_maximum_fusion.3), channel_id=1, source_target_pairs={{1,0},{2,1},{3,2},{4,3},{5,4},{6,5},{7,6},{8,7},{9,8},{10,9},{11,1... | collective-permute-start | bytes 442376 | tf_op jit(solution)/shard_map/ppermute | solution.py:31
  276.7 1.9 collective-permute-start.10
  278.6 0.2 collective-permute-done.11
  278.8 7.1 %collective-permute-done.10 = bf16[3,1,6,16,256]{4,3,2,1,0:T(8,128)(2,1)S(1)} collective-permute-done((bf16[3,1,6,16,256]{4,3,2,1,0:T(8,128)(2,1)S(1)}, bf16[3,1,6,16,256]{4,3,2,1,0:T(8,128)(2,1)S(1)}, u32[]{:S(2)}, u32[]{:S(2)}) %collective-permute-start.10) | collective-permute-done | bytes 147488 | tf_op jit(solution)/shard_map/ppermute | solution.py:28
  285.9 0.8 pad_maximum_fusion.1
  286.7 1.7 gather_fusion.2
  288.4 2.4 fusion.29
  290.8 1.8 fusion.34
  292.6 0.5 fusion.11
  293.2 0.9 fusion.40
  294.1 0.3 fusion.96
  294.4 1.9 collective-permute-start.12
  296.3 6.7 %collective-permute-start.13 = (bf16[3,6,16,256]{3,2,1,0:T(8,128)(2,1)S(1)}, bf16[3,6,16,256]{3,2,1,0:T(8,128)(2,1)S(1)}, u32[]{:S(2)}, u32[]{:S(2)}) collective-permute-start(bf16[3,6,16,256]{3,2,1,0:T(8,128)(2,1)S(1)} %get-tuple-element.19), channel_id=1, source_target_pairs={{1,0},{2,1},{3,2},{4,3},{5,4},{6,5},{7,6},{8,7},{9,8},{10,9},{11,1... | collective-permute-start | bytes 442376 | tf_op jit(solution)/shard_map/ppermute | solution.py:13
  303.0 0.6 collective-permute-done.12
  303.6 1.5 collective-permute-done.13
  305.2 6.2 %collective-permute-start.14 = (bf16[6,16,256]{2,1,0:T(8,128)(2,1)S(1)}, bf16[6,16,256]{2,1,0:T(8,128)(2,1)S(1)}, u32[]{:S(2)}, u32[]{:S(2)}) collective-permute-start(bf16[6,16,256]{2,1,0:T(8,128)(2,1)S(1)} %get-tuple-element.24), channel_id=1, source_target_pairs={{0,64},{64,128},{128,192},{192,256},{256,320},{320,384},{384,448},... | collective-permute-start | bytes 147464 | tf_op jit(solution)/shard_map/ppermute | solution.py:19
  311.4 1.9 collective-permute-start.15
  313.4 3.5 collective-permute-done.15
  316.8 0.7 multiply_reduce_fusion
  317.6 101.8 %psum.31 = f32[16]{0:T(128)} all-reduce(f32[16]{0:T(128)} %multiply_reduce_fusion), channel_id=1, replica_groups=mesh['lat'=8,'lon'=64] {'lat','lon'}, use_global_device_ids=true, to_apply=%region_7.8 | all-reduce | flops 16 | bytes 128 | tf_op jit(solution)/shard_map/psum | solution.py:101
  419.4 0.7 div.57
  420.1 1.7 multiply_subtract_fusion
  (58 shorter events, 0.6 us)
Async XLA Ops:
  0.6 33.6 %copy-start = (bf16[1,1,6,4,256,256]{5,4,3,2,1,0:T(8,128)(2,1)S(1)}, bf16[1,1,6,4,256,256]{5,4,3,2,1,0:T(8,128)(2,1)}, u32[]{:S(2)}) copy-start(bf16[1,1,6,4,256,256]{5,4,3,2,1,0:T(8,128)(2,1)} %param.10) | copy-start | bytes 9437188
  1.5 33.7 %copy-start.6 = (f32[6]{0:T(128)}, f32[6]{0:T(128)S(1)}, u32[]{:S(2)}) copy-start(f32[6]{0:T(128)S(1)} %compare_convert_fusion) | copy-start | bytes 76
  3.3 10.0 %collective-permute-start.1 = (bf16[1,1,6,16,256]{4,3,2,1,0:T(8,128)(2,1)S(1)}, bf16[1,1,6,16,256]{4,3,2,1,0:T(8,128)(2,1)S(1)}, u32[]{:S(2)}, u32[]{:S(2)}) collective-permute-start(bf16[1,1,6,16,256]{4,3,2,1,0:T(8,128)(2,1)S(1)} %multiply_convert_fusion), channel_id=1, source_target_pairs={{64,0},{128,64},{192,128},{256,192},{320,256},{384,320},{448,384},... | collective-permute-start | bytes 147464 | tf_op jit(solution)/shard_map/ppermute | solution.py:31
  10.2 3.1 collective-permute-start
  12.7 24.8 %copy-start.10 = (s32[24]{0:T(128)}, s32[24]{0:T(128)S(1)}, u32[]{:S(2)}) copy-start(s32[24]{0:T(128)S(1)} %get-tuple-element.16) | copy-start | bytes 292
  13.3 11.4 %collective-permute-start.3 = (bf16[3,1,6,16,256]{4,3,2,1,0:T(8,128)(2,1)S(1)}, bf16[3,1,6,16,256]{4,3,2,1,0:T(8,128)(2,1)S(1)}, u32[]{:S(2)}, u32[]{:S(2)}) collective-permute-start(bf16[3,1,6,16,256]{4,3,2,1,0:T(8,128)(2,1)S(1)} %pad_maximum_fusion.2), channel_id=1, source_target_pairs={{1,0},{2,1},{3,2},{4,3},{5,4},{6,5},{7,6},{8,7},{9,8},{10,9},{11,1... | collective-permute-start | bytes 442376 | tf_op jit(solution)/shard_map/ppermute | solution.py:31
  22.6 9.2 %collective-permute-start.2 = (bf16[3,1,6,16,256]{4,3,2,1,0:T(8,128)(2,1)S(1)}, bf16[3,1,6,16,256]{4,3,2,1,0:T(8,128)(2,1)S(1)}, u32[]{:S(2)}, u32[]{:S(2)}) collective-permute-start(bf16[3,1,6,16,256]{4,3,2,1,0:T(8,128)(2,1)S(1)} %pad_maximum_fusion.2), channel_id=1, source_target_pairs={{0,1},{1,2},{2,3},{3,4},{4,5},{5,6},{6,7},{7,8},{8,9},{9,10},{10,1... | collective-permute-start | bytes 442376 | tf_op jit(solution)/shard_map/ppermute | solution.py:28
  24.6 12.4 %copy-start.5 = (s32[1024]{0:T(1024)}, s32[1024]{0:T(1024)S(1)}, u32[]{:S(2)}) copy-start(s32[1024]{0:T(1024)S(1)} %pad_clamp_fusion) | copy-start | bytes 12292
  37.5 24.2 %copy-start.1 = (f32[1,1,6,16,256]{4,3,2,1,0:T(8,128)S(1)}, f32[1,1,6,16,256]{4,3,2,1,0:T(8,128)}, u32[]{:S(2)}) copy-start(f32[1,1,6,16,256]{4,3,2,1,0:T(8,128)} %param.7) | copy-start | bytes 294916
  37.5 24.2 %copy-start.7 = (f32[6]{0:T(128)S(1)}, f32[6]{0:T(128)}, u32[]{:S(2)}) copy-start(f32[6]{0:T(128)} %copy-done.6) | copy-start | bytes 76
  38.7 9.2 %collective-permute-start.4 = (bf16[3,6,16,256]{3,2,1,0:T(8,128)(2,1)S(1)}, bf16[3,6,16,256]{3,2,1,0:T(8,128)(2,1)S(1)}, u32[]{:S(2)}, u32[]{:S(2)}) collective-permute-start(bf16[3,6,16,256]{3,2,1,0:T(8,128)(2,1)S(1)} %get-tuple-element.20), channel_id=1, source_target_pairs={{63,0},{0,1},{1,2},{2,3},{3,4},{4,5},{5,6},{6,7},{7,8},{8,9},{9,10... | collective-permute-start | bytes 442376 | tf_op jit(solution)/shard_map/ppermute | solution.py:13
  40.7 8.8 %collective-permute-start.5 = (bf16[3,6,16,256]{3,2,1,0:T(8,128)(2,1)S(1)}, bf16[3,6,16,256]{3,2,1,0:T(8,128)(2,1)S(1)}, u32[]{:S(2)}, u32[]{:S(2)}) collective-permute-start(bf16[3,6,16,256]{3,2,1,0:T(8,128)(2,1)S(1)} %get-tuple-element.21), channel_id=1, source_target_pairs={{1,0},{2,1},{3,2},{4,3},{5,4},{6,5},{7,6},{8,7},{9,8},{10,9},{11,1... | collective-permute-start | bytes 442376 | tf_op jit(solution)/shard_map/ppermute | solution.py:13
  49.5 12.2 %copy-start.2 = (f32[3,6,16,256]{3,2,1,0:T(8,128)}, f32[3,6,16,256]{3,2,1,0:T(8,128)S(1)}, u32[]{:S(2)}) copy-start(f32[3,6,16,256]{3,2,1,0:T(8,128)S(1)} %get-tuple-element.13) | copy-start | bytes 884740
  49.5 8.6 %collective-permute-start.6 = (bf16[6,16,256]{2,1,0:T(8,128)(2,1)S(1)}, bf16[6,16,256]{2,1,0:T(8,128)(2,1)S(1)}, u32[]{:S(2)}, u32[]{:S(2)}) collective-permute-start(bf16[6,16,256]{2,1,0:T(8,128)(2,1)S(1)} %get-tuple-element.26), channel_id=1, source_target_pairs={{0,64},{64,128},{128,192},{192,256},{256,320},{320,384},{384,448},... | collective-permute-start | bytes 147464 | tf_op jit(solution)/shard_map/ppermute | solution.py:19
  56.3 5.4 %collective-permute-start.7 = (bf16[6,16,256]{2,1,0:T(8,128)(2,1)S(1)}, bf16[6,16,256]{2,1,0:T(8,128)(2,1)S(1)}, u32[]{:S(2)}, u32[]{:S(2)}) collective-permute-start(bf16[6,16,256]{2,1,0:T(8,128)(2,1)S(1)} %get-tuple-element.27), channel_id=1, source_target_pairs={{64,0},{128,64},{192,128},{256,192},{320,256},{384,320},{448,384},... | collective-permute-start | bytes 147464 | tf_op jit(solution)/shard_map/ppermute | solution.py:19
  164.6 0.5 copy-start.17
  165.1 1.6 copy-start.15
  266.0 0.6 copy-start.16
  266.6 0.6 copy-start.12
  267.8 18.9 %copy-start.4 = (bf16[1,1,6,16,256]{4,3,2,1,0:T(8,128)(2,1)}, bf16[1,1,6,16,256]{4,3,2,1,0:T(8,128)(2,1)S(1)}, u32[]{:S(2)}) copy-start(bf16[1,1,6,16,256]{4,3,2,1,0:T(8,128)(2,1)S(1)} %fusion.93) | copy-start | bytes 147460
  267.9 3.5 collective-permute-start.9
  268.5 2.8 collective-permute-start.8
  271.4 7.4 %collective-permute-start.11 = (bf16[3,1,6,16,256]{4,3,2,1,0:T(8,128)(2,1)S(1)}, bf16[3,1,6,16,256]{4,3,2,1,0:T(8,128)(2,1)S(1)}, u32[]{:S(2)}, u32[]{:S(2)}) collective-permute-start(bf16[3,1,6,16,256]{4,3,2,1,0:T(8,128)(2,1)S(1)} %pad_maximum_fusion.3), channel_id=1, source_target_pairs={{1,0},{2,1},{3,2},{4,3},{5,4},{6,5},{7,6},{8,7},{9,8},{10,9},{11,1... | collective-permute-start | bytes 442376 | tf_op jit(solution)/shard_map/ppermute | solution.py:31
  276.7 9.2 %collective-permute-start.10 = (bf16[3,1,6,16,256]{4,3,2,1,0:T(8,128)(2,1)S(1)}, bf16[3,1,6,16,256]{4,3,2,1,0:T(8,128)(2,1)S(1)}, u32[]{:S(2)}, u32[]{:S(2)}) collective-permute-start(bf16[3,1,6,16,256]{4,3,2,1,0:T(8,128)(2,1)S(1)} %pad_maximum_fusion.3), channel_id=1, source_target_pairs={{0,1},{1,2},{2,3},{3,4},{4,5},{5,6},{6,7},{7,8},{8,9},{9,10},{10,1... | collective-permute-start | bytes 442376 | tf_op jit(solution)/shard_map/ppermute | solution.py:28
  290.8 2.4 copy-start.11
  293.1 23.7 %copy-start.8 = (f32[6]{0:T(128)S(1)}, f32[6]{0:T(128)}, u32[]{:S(2)}) copy-start(f32[6]{0:T(128)} %copy-done.6) | copy-start | bytes 76
  293.1 23.7 %copy-start.13 = (f32[16]{0:T(128)S(1)}, f32[16]{0:T(128)}, u32[]{:S(2)}) copy-start(f32[16]{0:T(128)} %copy-done.12) | copy-start | bytes 196
  294.1 126.0 %copy-start.9 = (f32[6]{0:T(128)S(1)}, f32[6]{0:T(128)}, u32[]{:S(2)}) copy-start(f32[6]{0:T(128)} %copy-done.6) | copy-start | bytes 76
  294.1 126.0 %copy-start.14 = (f32[16]{0:T(128)S(1)}, f32[16]{0:T(128)}, u32[]{:S(2)}) copy-start(f32[16]{0:T(128)} %copy-done.12) | copy-start | bytes 196
  294.4 9.2 %collective-permute-start.12 = (bf16[3,6,16,256]{3,2,1,0:T(8,128)(2,1)S(1)}, bf16[3,6,16,256]{3,2,1,0:T(8,128)(2,1)S(1)}, u32[]{:S(2)}, u32[]{:S(2)}) collective-permute-start(bf16[3,6,16,256]{3,2,1,0:T(8,128)(2,1)S(1)} %get-tuple-element.18), channel_id=1, source_target_pairs={{63,0},{0,1},{1,2},{2,3},{3,4},{4,5},{5,6},{6,7},{7,8},{8,9},{9,10... | collective-permute-start | bytes 442376 | tf_op jit(solution)/shard_map/ppermute | solution.py:13
  296.3 8.8 %collective-permute-start.13 = (bf16[3,6,16,256]{3,2,1,0:T(8,128)(2,1)S(1)}, bf16[3,6,16,256]{3,2,1,0:T(8,128)(2,1)S(1)}, u32[]{:S(2)}, u32[]{:S(2)}) collective-permute-start(bf16[3,6,16,256]{3,2,1,0:T(8,128)(2,1)S(1)} %get-tuple-element.19), channel_id=1, source_target_pairs={{1,0},{2,1},{3,2},{4,3},{5,4},{6,5},{7,6},{8,7},{9,8},{10,9},{11,1... | collective-permute-start | bytes 442376 | tf_op jit(solution)/shard_map/ppermute | solution.py:13
  305.2 11.7 %copy-start.3 = (f32[3,6,16,256]{3,2,1,0:T(8,128)}, f32[3,6,16,256]{3,2,1,0:T(8,128)S(1)}, u32[]{:S(2)}) copy-start(f32[3,6,16,256]{3,2,1,0:T(8,128)S(1)} %get-tuple-element.7) | copy-start | bytes 884740
  305.2 8.2 %collective-permute-start.14 = (bf16[6,16,256]{2,1,0:T(8,128)(2,1)S(1)}, bf16[6,16,256]{2,1,0:T(8,128)(2,1)S(1)}, u32[]{:S(2)}, u32[]{:S(2)}) collective-permute-start(bf16[6,16,256]{2,1,0:T(8,128)(2,1)S(1)} %get-tuple-element.24), channel_id=1, source_target_pairs={{0,64},{64,128},{128,192},{192,256},{256,320},{320,384},{384,448},... | collective-permute-start | bytes 147464 | tf_op jit(solution)/shard_map/ppermute | solution.py:19
  311.4 5.4 %collective-permute-start.15 = (bf16[6,16,256]{2,1,0:T(8,128)(2,1)S(1)}, bf16[6,16,256]{2,1,0:T(8,128)(2,1)S(1)}, u32[]{:S(2)}, u32[]{:S(2)}) collective-permute-start(bf16[6,16,256]{2,1,0:T(8,128)(2,1)S(1)} %get-tuple-element.25), channel_id=1, source_target_pairs={{64,0},{128,64},{192,128},{256,192},{320,256},{384,320},{448,384},... | collective-permute-start | bytes 147464 | tf_op jit(solution)/shard_map/ppermute | solution.py:19
where the time goes:
time: 423 us; the launch traced here: 422 us
  blocking collectives  304 us (72%)
  starting transfers between devices  61.1 us (14%)
  waiting for transfers between devices  27.4 us (6%)
  other arithmetic  10.4 us (2%)
  matrix products  9.73 us (2%)
  local copies, waits for them, and re-layouts  7.63 us (2%)
    psum x2, blocking collectives, residual_total(): return lax.psum(inner(first, second), ('lat', 'lon'))  202 us
    psum x1, blocking collectives, body(): alpha = current / lax.psum(inner(direction, image), ('lat', 'lon'))  102 us
    ppermute x4, starting transfers between devices, with_halo(): lax.ppermute(lax.slice_in_dim(block, 0, width, axis=dim), axis, backward)  22.2 us
    ppermute x4, starting transfers between devices, from_behind(): return lax.ppermute(block, axis, route)  17.2 us
    ppermute x4, starting transfers between devices, from_behind_2(): lax.ppermute(value, axis, [(source, source + steps) for source in range(l...  16.8 us
    ppermute x4, waiting for transfers between devices, with_halo(): lax.ppermute(lax.slice_in_dim(block, block.shape[dim] - width, None, axis...  14.3 us
  transfers between devices with their start and end apart: 16, of which 11 were waited for; matrix products, arithmetic and copies ran while one was open for 1% of the time, Pallas kernels for 0%

commit v1 on v0

--- a/solution.py
+++ b/solution.py
@@ -98,7 +98,7 @@
         middle = placed[:, 1] + lon_back(placed[:, 2], 1) + lon_back(placed[:, 0], -1)
         total = middle[1] + lat_back(middle[2], 1) + lat_back(middle[0], -1)
         image = (back + total)[None, None] + nugget * direction
-        alpha = current / lax.psum(inner(direction, image), ("lat", "lon"))
+        alpha = current / lax.psum(lax.psum(inner(direction, image), "lon"), "lat")
         solution = solution + alpha[:, None] * direction
         residual = residual - alpha[:, None] * image
         if step + 1 < ITERS:

time: 423 us -> 625 us (1.48)
  blocking collectives: 304 us -> 508 us
    psum x1 -> x4, blocking collectives: 102 us -> 309 us  [body(): alpha = current / lax.psum(lax.psum(inner(direction, image), 'lon'), 'lat')]
  transfers between devices with their start and end apart: 16 -> 16, of which waited for: 11 -> 11; matrix products, arithmetic and copies ran while one was open for 1% -> 0% of each run, Pallas kernels for 0% -> 0%
where the time goes in v1:
time: 625 us; the launch traced here: 624 us
  blocking collectives  508 us (81%)
  starting transfers between devices  59.8 us (10%)
  waiting for transfers between devices  27.4 us (4%)
  other arithmetic  10.4 us (2%)
  matrix products  9.73 us (2%)
  local copies, waits for them, and re-layouts  7.66 us (1%)
    psum x4, blocking collectives, body(): alpha = current / lax.psum(lax.psum(inner(direction, image), 'lon'), 'lat')  309 us
    psum x2, blocking collectives, residual_total(): return lax.psum(inner(first, second), ('lat', 'lon'))  198 us
    ppermute x4, starting transfers between devices, with_halo(): lax.ppermute(lax.slice_in_dim(block, 0, width, axis=dim), axis, backward)  20.9 us
    ppermute x4, starting transfers between devices, from_behind(): return lax.ppermute(block, axis, route)  17.2 us
    ppermute x4, starting transfers between devices, from_behind_2(): lax.ppermute(value, axis, [(source, source + steps) for source in range(l...  16.8 us
    ppermute x4, waiting for transfers between devices, with_halo(): lax.ppermute(lax.slice_in_dim(block, block.shape[dim] - width, None, axis...  14.3 us
  transfers between devices with their start and end apart: 16, of which 11 were waited for; matrix products, arithmetic and copies ran while one was open for 0% of the time, Pallas kernels for 0%

profile of v1, /device:TPU:1, one launch (start us, length us, event | category | flops | bytes accessed | tf_op | source)
XLA Modules:
  0.0 624.4 jit_solution(14306926299640977468)
XLA Ops:
  1.5 0.8 copy.60
  2.3 1.0 multiply_convert_fusion
  3.3 6.9 %collective-permute-start.1 = (bf16[1,1,6,16,256]{4,3,2,1,0:T(8,128)(2,1)S(1)}, bf16[1,1,6,16,256]{4,3,2,1,0:T(8,128)(2,1)S(1)}, u32[]{:S(2)}, u32[]{:S(2)}) collective-permute-start(bf16[1,1,6,16,256]{4,3,2,1,0:T(8,128)(2,1)S(1)} %multiply_convert_fusion), channel_id=1, source_target_pairs={{64,0},{128,64},{192,128},{256,192},{320,256},{384,320},{448,384},... | collective-permute-start | bytes 147464 | tf_op jit(solution)/shard_map/ppermute | solution.py:31
  10.2 0.7 compare_select_fusion.1
  10.8 0.1 copy.22
  11.0 1.4 gather_fusion
  12.5 0.1 copy.24
  12.8 0.1 copy.25
  12.9 0.1 copy.23
  13.1 0.1 copy.30
  13.3 9.3 %collective-permute-start.3 = (bf16[3,1,6,16,256]{4,3,2,1,0:T(8,128)(2,1)S(1)}, bf16[3,1,6,16,256]{4,3,2,1,0:T(8,128)(2,1)S(1)}, u32[]{:S(2)}, u32[]{:S(2)}) collective-permute-start(bf16[3,1,6,16,256]{4,3,2,1,0:T(8,128)(2,1)S(1)} %pad_maximum_fusion.2), channel_id=1, source_target_pairs={{1,0},{2,1},{3,2},{4,3},{5,4},{6,5},{7,6},{8,7},{9,8},{10,9},{11,1... | collective-permute-start | bytes 442376 | tf_op jit(solution)/shard_map/ppermute | solution.py:31
  22.6 1.9 collective-permute-start.2
  24.6 0.1 collective-permute-done.3
  24.7 7.1 %collective-permute-done.2 = bf16[3,1,6,16,256]{4,3,2,1,0:T(8,128)(2,1)S(1)} collective-permute-done((bf16[3,1,6,16,256]{4,3,2,1,0:T(8,128)(2,1)S(1)}, bf16[3,1,6,16,256]{4,3,2,1,0:T(8,128)(2,1)S(1)}, u32[]{:S(2)}, u32[]{:S(2)}) %collective-permute-start.2) | collective-permute-done | bytes 147488 | tf_op jit(solution)/shard_map/ppermute | solution.py:28
  31.8 0.8 pad_maximum_fusion
  32.6 1.6 gather_fusion.1
  34.2 0.9 fusion.26
  35.1 1.8 fusion.35
  37.0 0.5 fusion.8
  37.5 0.9 fusion.42
  38.4 0.3 fusion.99
  38.7 1.9 collective-permute-start.4
  40.7 6.7 %collective-permute-start.5 = (bf16[3,6,16,256]{3,2,1,0:T(8,128)(2,1)S(1)}, bf16[3,6,16,256]{3,2,1,0:T(8,128)(2,1)S(1)}, u32[]{:S(2)}, u32[]{:S(2)}) collective-permute-start(bf16[3,6,16,256]{3,2,1,0:T(8,128)(2,1)S(1)} %get-tuple-element.19), channel_id=1, source_target_pairs={{1,0},{2,1},{3,2},{4,3},{5,4},{6,5},{7,6},{8,7},{9,8},{10,9},{11,1... | collective-permute-start | bytes 442376 | tf_op jit(solution)/shard_map/ppermute | solution.py:13
  47.4 0.6 collective-permute-done.4
  47.9 1.5 collective-permute-done.5
  49.5 6.7 %collective-permute-start.6 = (bf16[6,16,256]{2,1,0:T(8,128)(2,1)S(1)}, bf16[6,16,256]{2,1,0:T(8,128)(2,1)S(1)}, u32[]{:S(2)}, u32[]{:S(2)}) collective-permute-start(bf16[6,16,256]{2,1,0:T(8,128)(2,1)S(1)} %get-tuple-element.24), channel_id=1, source_target_pairs={{0,64},{64,128},{128,192},{192,256},{256,320},{320,384},{384,448},... | collective-permute-start | bytes 147464 | tf_op jit(solution)/shard_map/ppermute | solution.py:19
  56.2 1.9 collective-permute-start.7
  58.2 3.5 collective-permute-done.7
  61.7 0.2 fusion.49
  61.9 116.3 %psum.43 = f32[16]{0:T(128)S(1)} all-reduce(f32[16]{0:T(128)S(1)} %get-tuple-element.2), channel_id=1, replica_groups=mesh['lat'=8,'lon'=64] {'lon'}, use_global_device_ids=true, to_apply=%region_3.4 | all-reduce | flops 16 | bytes 128 | tf_op jit(solution)/shard_map/psum | solution.py:101
  178.2 38.2 %psum.44 = f32[16]{0:T(128)S(1)} all-reduce(f32[16]{0:T(128)S(1)} %psum.43), channel_id=1, replica_groups=mesh['lat'=8,'lon'=64] {'lat'}, use_global_device_ids=true, to_apply=%region_4.5 | all-reduce | flops 16 | bytes 128 | tf_op jit(solution)/shard_map/psum | solution.py:101
  216.3 98.7 %psum.42 = f32[16]{0:T(128)S(1)} all-reduce(f32[16]{0:T(128)S(1)} %get-tuple-element.3), channel_id=1, replica_groups=mesh['lat'=8,'lon'=64] {'lat','lon'}, use_global_device_ids=true, to_apply=%region_1.2 | all-reduce | flops 16 | bytes 128 | tf_op jit(solution)/shard_map/psum | solution.py:72
  315.0 0.5 copy-done.17
  315.6 1.6 fusion.51
  317.2 99.7 %psum.45 = f32[16]{0:T(128)S(1)} all-reduce(f32[16]{0:T(128)} %get-tuple-element.8), channel_id=1, replica_groups=mesh['lat'=8,'lon'=64] {'lat','lon'}, use_global_device_ids=true, to_apply=%region_6.7 | all-reduce | flops 16 | bytes 128 | tf_op jit(solution)/shard_map/psum | solution.py:72
  416.8 0.6 div.56
  417.5 0.6 copy-done.12
  418.1 0.7 fusion.93
  418.8 0.7 collective-permute-start.9
  419.5 1.1 collective-permute-start.8
  420.6 1.8 collective-permute-done.9
  422.4 4.0 collective-permute-start.11
  426.4 1.9 collective-permute-start.10
  428.3 0.2 collective-permute-done.11
  428.4 7.1 %collective-permute-done.10 = bf16[3,1,6,16,256]{4,3,2,1,0:T(8,128)(2,1)S(1)} collective-permute-done((bf16[3,1,6,16,256]{4,3,2,1,0:T(8,128)(2,1)S(1)}, bf16[3,1,6,16,256]{4,3,2,1,0:T(8,128)(2,1)S(1)}, u32[]{:S(2)}, u32[]{:S(2)}) %collective-permute-start.10) | collective-permute-done | bytes 147488 | tf_op jit(solution)/shard_map/ppermute | solution.py:28
  435.6 0.8 pad_maximum_fusion.1
  436.4 1.7 gather_fusion.2
  438.1 2.4 fusion.29
  440.4 1.8 fusion.34
  442.3 0.5 fusion.11
  442.8 0.9 fusion.40
  443.7 0.3 fusion.96
  444.0 1.9 collective-permute-start.12
  446.0 6.7 %collective-permute-start.13 = (bf16[3,6,16,256]{3,2,1,0:T(8,128)(2,1)S(1)}, bf16[3,6,16,256]{3,2,1,0:T(8,128)(2,1)S(1)}, u32[]{:S(2)}, u32[]{:S(2)}) collective-permute-start(bf16[3,6,16,256]{3,2,1,0:T(8,128)(2,1)S(1)} %get-tuple-element.17), channel_id=1, source_target_pairs={{1,0},{2,1},{3,2},{4,3},{5,4},{6,5},{7,6},{8,7},{9,8},{10,9},{11,1... | collective-permute-start | bytes 442376 | tf_op jit(solution)/shard_map/ppermute | solution.py:13
  452.7 0.6 collective-permute-done.12
  453.2 1.5 collective-permute-done.13
  454.8 6.2 collective-permute-start.14
  461.1 1.9 collective-permute-start.15
  463.0 3.5 collective-permute-done.15
  466.5 0.7 multiply_reduce_fusion
  467.2 116.9 %psum.46 = f32[16]{0:T(128)} all-reduce(f32[16]{0:T(128)} %multiply_reduce_fusion), channel_id=1, replica_groups=mesh['lat'=8,'lon'=64] {'lon'}, use_global_device_ids=true, to_apply=%region_8.9 | all-reduce | flops 16 | bytes 128 | tf_op jit(solution)/shard_map/psum | solution.py:101
  584.1 37.9 %psum.47 = f32[16]{0:T(128)} all-reduce(f32[16]{0:T(128)} %psum.46), channel_id=1, replica_groups=mesh['lat'=8,'lon'=64] {'lat'}, use_global_device_ids=true, to_apply=%region_9.10 | all-reduce | flops 16 | bytes 128 | tf_op jit(solution)/shard_map/psum | solution.py:101
  622.0 0.7 div.57
  622.7 1.7 multiply_subtract_fusion
  (61 shorter events, 0.8 us)
Async XLA Ops:
  0.6 33.6 %copy-start = (bf16[1,1,6,4,256,256]{5,4,3,2,1,0:T(8,128)(2,1)S(1)}, bf16[1,1,6,4,256,256]{5,4,3,2,1,0:T(8,128)(2,1)}, u32[]{:S(2)}) copy-start(bf16[1,1,6,4,256,256]{5,4,3,2,1,0:T(8,128)(2,1)} %param.10) | copy-start | bytes 9437188
  1.5 33.7 %copy-start.6 = (f32[6]{0:T(128)}, f32[6]{0:T(128)S(1)}, u32[]{:S(2)}) copy-start(f32[6]{0:T(128)S(1)} %compare_convert_fusion) | copy-start | bytes 76
  3.3 10.0 %collective-permute-start.1 = (bf16[1,1,6,16,256]{4,3,2,1,0:T(8,128)(2,1)S(1)}, bf16[1,1,6,16,256]{4,3,2,1,0:T(8,128)(2,1)S(1)}, u32[]{:S(2)}, u32[]{:S(2)}) collective-permute-start(bf16[1,1,6,16,256]{4,3,2,1,0:T(8,128)(2,1)S(1)} %multiply_convert_fusion), channel_id=1, source_target_pairs={{64,0},{128,64},{192,128},{256,192},{320,256},{384,320},{448,384},... | collective-permute-start | bytes 147464 | tf_op jit(solution)/shard_map/ppermute | solution.py:31
  10.2 3.1 collective-permute-start
  12.7 24.8 %copy-start.10 = (s32[24]{0:T(128)}, s32[24]{0:T(128)S(1)}, u32[]{:S(2)}) copy-start(s32[24]{0:T(128)S(1)} %get-tuple-element.14) | copy-start | bytes 292
  13.3 11.4 %collective-permute-start.3 = (bf16[3,1,6,16,256]{4,3,2,1,0:T(8,128)(2,1)S(1)}, bf16[3,1,6,16,256]{4,3,2,1,0:T(8,128)(2,1)S(1)}, u32[]{:S(2)}, u32[]{:S(2)}) collective-permute-start(bf16[3,1,6,16,256]{4,3,2,1,0:T(8,128)(2,1)S(1)} %pad_maximum_fusion.2), channel_id=1, source_target_pairs={{1,0},{2,1},{3,2},{4,3},{5,4},{6,5},{7,6},{8,7},{9,8},{10,9},{11,1... | collective-permute-start | bytes 442376 | tf_op jit(solution)/shard_map/ppermute | solution.py:31
  22.6 9.2 %collective-permute-start.2 = (bf16[3,1,6,16,256]{4,3,2,1,0:T(8,128)(2,1)S(1)}, bf16[3,1,6,16,256]{4,3,2,1,0:T(8,128)(2,1)S(1)}, u32[]{:S(2)}, u32[]{:S(2)}) collective-permute-start(bf16[3,1,6,16,256]{4,3,2,1,0:T(8,128)(2,1)S(1)} %pad_maximum_fusion.2), channel_id=1, source_target_pairs={{0,1},{1,2},{2,3},{3,4},{4,5},{5,6},{6,7},{7,8},{8,9},{9,10},{10,1... | collective-permute-start | bytes 442376 | tf_op jit(solution)/shard_map/ppermute | solution.py:28
  24.6 12.4 %copy-start.5 = (s32[1024]{0:T(1024)}, s32[1024]{0:T(1024)S(1)}, u32[]{:S(2)}) copy-start(s32[1024]{0:T(1024)S(1)} %pad_clamp_fusion) | copy-start | bytes 12292
  37.5 24.2 %copy-start.1 = (f32[1,1,6,16,256]{4,3,2,1,0:T(8,128)S(1)}, f32[1,1,6,16,256]{4,3,2,1,0:T(8,128)}, u32[]{:S(2)}) copy-start(f32[1,1,6,16,256]{4,3,2,1,0:T(8,128)} %param.7) | copy-start | bytes 294916
  37.5 24.2 %copy-start.7 = (f32[6]{0:T(128)S(1)}, f32[6]{0:T(128)}, u32[]{:S(2)}) copy-start(f32[6]{0:T(128)} %copy-done.6) | copy-start | bytes 76
  38.7 9.2 %collective-permute-start.4 = (bf16[3,6,16,256]{3,2,1,0:T(8,128)(2,1)S(1)}, bf16[3,6,16,256]{3,2,1,0:T(8,128)(2,1)S(1)}, u32[]{:S(2)}, u32[]{:S(2)}) collective-permute-start(bf16[3,6,16,256]{3,2,1,0:T(8,128)(2,1)S(1)} %get-tuple-element.18), channel_id=1, source_target_pairs={{63,0},{0,1},{1,2},{2,3},{3,4},{4,5},{5,6},{6,7},{7,8},{8,9},{9,10... | collective-permute-start | bytes 442376 | tf_op jit(solution)/shard_map/ppermute | solution.py:13
  40.7 8.8 %collective-permute-start.5 = (bf16[3,6,16,256]{3,2,1,0:T(8,128)(2,1)S(1)}, bf16[3,6,16,256]{3,2,1,0:T(8,128)(2,1)S(1)}, u32[]{:S(2)}, u32[]{:S(2)}) collective-permute-start(bf16[3,6,16,256]{3,2,1,0:T(8,128)(2,1)S(1)} %get-tuple-element.19), channel_id=1, source_target_pairs={{1,0},{2,1},{3,2},{4,3},{5,4},{6,5},{7,6},{8,7},{9,8},{10,9},{11,1... | collective-permute-start | bytes 442376 | tf_op jit(solution)/shard_map/ppermute | solution.py:13
  49.5 12.2 %copy-start.2 = (f32[3,6,16,256]{3,2,1,0:T(8,128)}, f32[3,6,16,256]{3,2,1,0:T(8,128)S(1)}, u32[]{:S(2)}) copy-start(f32[3,6,16,256]{3,2,1,0:T(8,128)S(1)} %get-tuple-element.11) | copy-start | bytes 884740
  49.5 8.6 %collective-permute-start.6 = (bf16[6,16,256]{2,1,0:T(8,128)(2,1)S(1)}, bf16[6,16,256]{2,1,0:T(8,128)(2,1)S(1)}, u32[]{:S(2)}, u32[]{:S(2)}) collective-permute-start(bf16[6,16,256]{2,1,0:T(8,128)(2,1)S(1)} %get-tuple-element.24), channel_id=1, source_target_pairs={{0,64},{64,128},{128,192},{192,256},{256,320},{320,384},{384,448},... | collective-permute-start | bytes 147464 | tf_op jit(solution)/shard_map/ppermute | solution.py:19
  56.2 5.4 collective-permute-start.7
  315.0 0.5 copy-start.17
  315.6 1.6 copy-start.15
  416.8 0.6 copy-start.16
  417.5 0.6 copy-start.12
  418.8 17.6 %copy-start.4 = (bf16[1,1,6,16,256]{4,3,2,1,0:T(8,128)(2,1)}, bf16[1,1,6,16,256]{4,3,2,1,0:T(8,128)(2,1)S(1)}, u32[]{:S(2)}) copy-start(bf16[1,1,6,16,256]{4,3,2,1,0:T(8,128)(2,1)S(1)} %fusion.93) | copy-start | bytes 147460
  418.8 3.5 collective-permute-start.9
  419.5 2.8 collective-permute-start.8
  422.4 6.1 collective-permute-start.11
  426.4 9.2 %collective-permute-start.10 = (bf16[3,1,6,16,256]{4,3,2,1,0:T(8,128)(2,1)S(1)}, bf16[3,1,6,16,256]{4,3,2,1,0:T(8,128)(2,1)S(1)}, u32[]{:S(2)}, u32[]{:S(2)}) collective-permute-start(bf16[3,1,6,16,256]{4,3,2,1,0:T(8,128)(2,1)S(1)} %pad_maximum_fusion.3), channel_id=1, source_target_pairs={{0,1},{1,2},{2,3},{3,4},{4,5},{5,6},{6,7},{7,8},{8,9},{9,10},{10,1... | collective-permute-start | bytes 442376 | tf_op jit(solution)/shard_map/ppermute | solution.py:28
  440.4 2.4 copy-start.11
  442.8 23.7 %copy-start.8 = (f32[6]{0:T(128)S(1)}, f32[6]{0:T(128)}, u32[]{:S(2)}) copy-start(f32[6]{0:T(128)} %copy-done.6) | copy-start | bytes 76
  442.8 23.7 %copy-start.13 = (f32[16]{0:T(128)S(1)}, f32[16]{0:T(128)}, u32[]{:S(2)}) copy-start(f32[16]{0:T(128)} %copy-done.12) | copy-start | bytes 196
  443.7 179.0 %copy-start.9 = (f32[6]{0:T(128)S(1)}, f32[6]{0:T(128)}, u32[]{:S(2)}) copy-start(f32[6]{0:T(128)} %copy-done.6) | copy-start | bytes 76
  443.7 179.0 %copy-start.14 = (f32[16]{0:T(128)S(1)}, f32[16]{0:T(128)}, u32[]{:S(2)}) copy-start(f32[16]{0:T(128)} %copy-done.12) | copy-start | bytes 196
  444.0 9.2 %collective-permute-start.12 = (bf16[3,6,16,256]{3,2,1,0:T(8,128)(2,1)S(1)}, bf16[3,6,16,256]{3,2,1,0:T(8,128)(2,1)S(1)}, u32[]{:S(2)}, u32[]{:S(2)}) collective-permute-start(bf16[3,6,16,256]{3,2,1,0:T(8,128)(2,1)S(1)} %get-tuple-element.16), channel_id=1, source_target_pairs={{63,0},{0,1},{1,2},{2,3},{3,4},{4,5},{5,6},{6,7},{7,8},{8,9},{9,10... | collective-permute-start | bytes 442376 | tf_op jit(solution)/shard_map/ppermute | solution.py:13
  446.0 8.8 %collective-permute-start.13 = (bf16[3,6,16,256]{3,2,1,0:T(8,128)(2,1)S(1)}, bf16[3,6,16,256]{3,2,1,0:T(8,128)(2,1)S(1)}, u32[]{:S(2)}, u32[]{:S(2)}) collective-permute-start(bf16[3,6,16,256]{3,2,1,0:T(8,128)(2,1)S(1)} %get-tuple-element.17), channel_id=1, source_target_pairs={{1,0},{2,1},{3,2},{4,3},{5,4},{6,5},{7,6},{8,7},{9,8},{10,9},{11,1... | collective-permute-start | bytes 442376 | tf_op jit(solution)/shard_map/ppermute | solution.py:13
  454.8 11.7 %copy-start.3 = (f32[3,6,16,256]{3,2,1,0:T(8,128)}, f32[3,6,16,256]{3,2,1,0:T(8,128)S(1)}, u32[]{:S(2)}) copy-start(f32[3,6,16,256]{3,2,1,0:T(8,128)S(1)} %get-tuple-element.5) | copy-start | bytes 884740
  454.8 8.2 %collective-permute-start.14 = (bf16[6,16,256]{2,1,0:T(8,128)(2,1)S(1)}, bf16[6,16,256]{2,1,0:T(8,128)(2,1)S(1)}, u32[]{:S(2)}, u32[]{:S(2)}) collective-permute-start(bf16[6,16,256]{2,1,0:T(8,128)(2,1)S(1)} %get-tuple-element.22), channel_id=1, source_target_pairs={{0,64},{64,128},{128,192},{192,256},{256,320},{320,384},{384,448},... | collective-permute-start | bytes 147464 | tf_op jit(solution)/shard_map/ppermute | solution.py:19
  461.1 5.4 collective-permute-start.15
